TPU v7x, 32 devices: a whole 2x2x4 slice. The times are simulated.
32 devices in a mesh: row: 4 (over x, core), col: 8 (over z, y).
Axes of the slice: x: 2, y: 2, z: 4, core: 2. Of those that a mesh axis runs over, the one named last changes fastest.
Arguments:
- block_in: bfloat16 [4096, 2048], P('col', 'row'), may hold values from -6 to 6
- cotangent: bfloat16 [4096, 2048], P('col', 'row'), may hold values from -6 to 6
- segments: int32 [4096], P('row'), may hold values from 0 to 31, never falling along the last dimension, each value on 1 to 1024 neighbouring positions
- w_query: bfloat16 [2048, 2048], P('row', 'col'), may hold values from -0.125 to 0.125
- w_key: bfloat16 [2048, 2048], P('row', 'col'), may hold values from -0.125 to 0.125
- w_value: bfloat16 [2048, 4096], P('row', 'col'), may hold values from -0.125 to 0.125
- w_gate: bfloat16 [2048, 4096], P('row', 'col'), may hold values from -0.125 to 0.125
- w_out: bfloat16 [4096, 2048], P('col', 'row'), may hold values from -0.09375 to 0.09375
- w_up: bfloat16 [2048, 4096], P('row', 'col'), may hold values from -0.125 to 0.125
- w_down: bfloat16 [4096, 2048], P('col', 'row'), may hold values from -0.09375 to 0.09375
- retention_norm_gain: float32 [2048], P('row'), may hold values from 0.25 to 1.75
- retention_norm_bias: float32 [2048], P('row'), may hold values from -3 to 3
- feedforward_norm_gain: float32 [2048], P('row'), may hold values from 0.25 to 1.75
- feedforward_norm_bias: float32 [2048], P('row'), may hold values from -3 to 3
Outputs:
- block_out: bfloat16 [4096, 2048], P('col', 'row')
- grad_in: float32 [4096, 2048], P('col', 'row')
- grad_query: float32 [2048, 2048], P('row', 'col')
- grad_key: float32 [2048, 2048], P('row', 'col')
- grad_value: float32 [2048, 4096], P('row', 'col')
- grad_gate: float32 [2048, 4096], P('row', 'col')
- grad_out: float32 [4096, 2048], P('col', 'row')
- grad_up: float32 [2048, 4096], P('row', 'col')
- grad_down: float32 [4096, 2048], P('col', 'row')
- grad_attn_gain: float32 [2048], P('row')
- grad_attn_bias: float32 [2048], P('row')
- grad_ffn_gain: float32 [2048], P('row')
- grad_ffn_bias: float32 [2048], P('row')
Inputs may be any that keep to these rules, and one draw needn't show every extreme that they name: `segments`: segment numbers never fall along the tokens; a document holds 1 to 1024 tokens.
All inputs are finite; a program needn't handle non-finite values.
Results may differ from a plain program's by a relative error of at most 0.014.
The roundings to bfloat16 on the way count: a program that leaves them out, or rounds other values in their place, can miss the bound.
Values may be sent and summed in bfloat16 or wider, within the bound.
No kernel may reach another device: no remote copies, remote signals or barrier semaphores. Data moves between devices by JAX's collectives and lax.ppermute only.
A program may use at most 320 MiB of HBM per device.

v0:
```python
import jax
import jax.numpy as jnp
from jax import lax
from jax.sharding import Mesh
from jax.sharding import PartitionSpec as P

HEADS = 8
EPS_NORM = 1e-05
EPS_GROUP = 0.25
ROW = ("x", "k")
GROUP = ("x", "k", "y")
EVERY = ("x", "k", "z", "y")
F32 = jnp.float32
BF16 = jnp.bfloat16


def dot(left, right, over):
    return lax.dot_general(left, right, (over, ((), ())), preferred_element_type=F32)


def swap(value, mask):
    return lax.ppermute(value, GROUP, [(i, i ^ mask) for i in range(8)])


def group_gather(part):
    near = jnp.stack([part, swap(part, 1), swap(part, 4), swap(part, 5)])
    near = near.reshape((2, 1, 2) + part.shape)
    return jnp.concatenate([near, swap(near, 2)], axis=1).reshape((-1,) + part.shape[1:])


def group_reduce(total):
    blocks = total.reshape(2, 2, 2, total.shape[0] // 8, total.shape[1])
    pair = (blocks[:, 0] + swap(blocks[:, 1].astype(BF16), 2).astype(F32)).astype(BF16)
    own = pair[0, 0].astype(F32)
    for i, j in ((0, 1), (1, 0), (1, 1)):
        own = own + swap(pair[i, j], 4 * i + j).astype(F32)
    return own


def row_exchange(parts):
    return lax.all_to_all(parts, ROW, split_axis=0, concat_axis=0, tiled=True)


def to_tokens(part):
    tokens, width = part.shape
    moved = row_exchange(part.reshape(4, tokens // 4, width))
    return moved.transpose(1, 0, 2).reshape(tokens // 4, 4 * width)


def from_tokens(part):
    tokens, width = part.shape
    moved = row_exchange(part.reshape(tokens, 4, width // 4).transpose(1, 0, 2))
    return moved.reshape(4 * tokens, width // 4)


def head_order(count):
    units = count // HEADS
    j = lax.iota(jnp.int32, count)
    target = j % HEADS * units + j // HEADS
    return (target[:, None] == lax.iota(jnp.int32, count)[None, :]).astype(BF16)


def layernorm(value, gain, bias):
    mean = jnp.mean(value, axis=1, keepdims=True)
    centered = value - mean
    inverse = lax.rsqrt(jnp.mean(centered * centered, axis=1, keepdims=True) + EPS_NORM)
    hat = centered * inverse
    return (hat, inverse, (hat * gain + bias).astype(BF16))


def layernorm_back(grad, hat, inverse, gain):
    scaled = grad * gain
    first = jnp.mean(scaled, axis=1, keepdims=True)
    second = jnp.mean(scaled * hat, axis=1, keepdims=True)
    return (
        inverse * (scaled - first - hat * second),
        jnp.sum(grad * hat, axis=0),
        jnp.sum(grad, axis=0),
    )


def gelu_exact(value):
    return jax.nn.gelu(value, approximate=False)


def body(
    block_in,
    cotangent,
    segments,
    w_query,
    w_key,
    w_value,
    w_gate,
    w_out,
    w_up,
    w_down,
    retention_norm_gain,
    retention_norm_bias,
    feedforward_norm_gain,
    feedforward_norm_bias,
):
    depth = lax.axis_size("z")
    part = block_in.shape[1]
    width = 4 * part
    own = lax.axis_index(GROUP)
    plane = lax.axis_index("z")
    tokens = block_in.shape[0] // 4
    seq = 8 * tokens
    kq = w_query.shape[1] // HEADS
    kv = w_value.shape[1] // HEADS
    order_q = head_order(w_query.shape[1])
    order_v = head_order(w_value.shape[1])

    def by_head(weight, order):
        return dot(order, weight, ((0,), (1,))).astype(BF16).reshape(HEADS, -1, part)

    send_qkv = jnp.concatenate(
        [by_head(w_query, order_q), by_head(w_key, order_q), by_head(w_value, order_v)], axis=1
    )
    send_go = jnp.concatenate(
        [
            by_head(w_gate, order_v),
            dot(order_v, w_out, ((0,), (0,))).astype(BF16).reshape(HEADS, -1, part),
        ],
        axis=1,
    )

    def to_heads(send):
        got = lax.all_to_all(send, GROUP, split_axis=0, concat_axis=0, tiled=True)
        got = got.reshape(4, 2, send.shape[1], part).transpose(1, 2, 0, 3)
        return got.reshape(2, send.shape[1], width)

    got_qkv = to_heads(send_qkv)
    got_go = to_heads(send_go)
    mine_qkv = jnp.concatenate(
        [
            got_qkv[:, :kq].reshape(2 * kq, width),
            got_qkv[:, kq : 2 * kq].reshape(2 * kq, width),
            got_qkv[:, 2 * kq :].reshape(2 * kv, width),
        ],
        axis=0,
    )
    mine_go = jnp.concatenate(
        [got_go[:, :kv].reshape(2 * kv, width), got_go[:, kv:].reshape(2 * kv, width)], axis=0
    )

    def to_units(weight):
        got = row_exchange(weight.reshape(4, -1, part))
        return got.transpose(1, 0, 2).reshape(-1, width)

    mine_up = to_units(w_up.T)
    mine_down = to_units(w_down)

    def planes(mine):
        return lax.all_gather(mine, "z", axis=0, tiled=True)

    all_qkv = planes(mine_qkv)
    all_go = planes(mine_go).reshape(depth, 4 * kv, width)
    wt_gate = all_go[:, : 2 * kv].reshape(-1, width)
    wt_out = all_go[:, 2 * kv :].reshape(-1, width)
    wt_up = planes(mine_up)
    wt_down = planes(mine_down)
    params = lax.all_gather(
        jnp.stack(
            [retention_norm_gain, retention_norm_bias, feedforward_norm_gain, feedforward_norm_bias]
        ),
        ROW,
        axis=1,
        tiled=True,
    )
    stream = to_tokens(block_in).astype(F32)
    cot_own = to_tokens(cotangent)
    hat_one, inv_one, norm_one = layernorm(stream, params[0], params[1])
    x_one = group_gather(norm_one)
    cot = group_gather(cot_own)
    segs = lax.all_gather(segments, ROW, axis=0, tiled=True).reshape(depth, 8, tokens)
    ids = lax.iota(jnp.int32, 8) ^ own
    ids = ids % 2 * 4 + ids // 2
    picked = (ids[:, None] == lax.iota(jnp.int32, 8)[None, :])[:, :, None]
    here = (lax.iota(jnp.int32, depth) == plane)[:, None, None]
    seg_plane = jnp.sum(jnp.where(here, segs, 0), axis=0)
    seg = jnp.sum(jnp.where(picked, seg_plane[None], 0), axis=1).reshape(seq)
    pos = (ids[:, None] * tokens + lax.iota(jnp.int32, tokens)[None, :]).reshape(seq)
    loggam = jnp.log1p(-jnp.exp2(-5.0 - own.astype(F32)))
    gap = pos[:, None] - pos[None, :]
    inside = (gap >= 0) & (seg[:, None] == seg[None, :])
    decay = jnp.where(inside, jnp.exp(jnp.maximum(gap, 0).astype(F32) * loggam), F32(0.0))
    scale = (kq * 2 * depth) ** (-0.5)
    qkv = dot(all_qkv, x_one, ((1,), (1,))).astype(BF16).reshape(depth, -1, seq)
    query = qkv[:, : 2 * kq].reshape(-1, seq)
    keys = qkv[:, 2 * kq : 4 * kq].reshape(-1, seq)
    values = qkv[:, 4 * kq :].reshape(-1, seq)
    raw = dot(query, keys, ((0,), (0,)))
    weights = (raw * scale * decay).astype(BF16)
    retained = dot(values, weights, ((1,), (1,)))
    centered = retained - jnp.mean(retained, axis=0, keepdims=True)
    inv_group = lax.rsqrt(jnp.mean(centered * centered, axis=0, keepdims=True) + EPS_GROUP)
    normed = centered * inv_group
    normed_low = normed.astype(BF16).astype(F32)
    gate = dot(wt_gate, x_one, ((1,), (1,)))
    sigma = jax.nn.sigmoid(gate)
    swish = gate * sigma
    hidden = (swish * normed_low).astype(BF16)
    middle = stream + group_reduce(dot(hidden, wt_out, ((0,), (0,))))
    hat_two, inv_two, norm_two = layernorm(middle, params[2], params[3])
    x_two = group_gather(norm_two)
    pre = dot(wt_up, x_two, ((1,), (1,)))
    act_wide, act_pull = jax.vjp(gelu_exact, pre)
    act = act_wide.astype(BF16)
    grad_act = dot(wt_down, cot, ((1,), (1,)))
    grad_pre = act_pull(grad_act)[0].astype(BF16)
    grad_two = group_reduce(dot(grad_pre, wt_up, ((0,), (0,))))
    ffn = group_reduce(dot(act, wt_down, ((0,), (0,))))
    block_out = from_tokens((middle + ffn).astype(BF16))

    def home(full):
        return lax.psum_scatter(full.astype(BF16), "z", scatter_dimension=0, tiled=True)

    def from_units(mine):
        send = mine.reshape(-1, 4, part).transpose(1, 0, 2)
        return row_exchange(send).reshape(-1, part)

    grad_down = from_units(home(dot(act, cot, ((1,), (0,))))).astype(F32)
    grad_up = from_units(home(dot(grad_pre, x_two, ((1,), (0,))))).T.astype(F32)
    back_two, grad_ffn_gain, grad_ffn_bias = layernorm_back(grad_two, hat_two, inv_two, params[2])
    grad_mid = cot_own.astype(F32) + back_two
    x_mid = group_gather(grad_mid.astype(BF16))
    grad_out_full = dot(hidden, x_mid, ((1,), (0,)))
    grad_hidden = dot(wt_out, x_mid, ((1,), (1,)))
    grad_gate = (grad_hidden * normed_low * (sigma * (1.0 + gate * (1.0 - sigma)))).astype(BF16)
    grad_normed = (grad_hidden * swish).astype(BF16).astype(F32)
    grad_ret = (
        inv_group
        * (
            grad_normed
            - jnp.mean(grad_normed, axis=0, keepdims=True)
            - normed * jnp.mean(grad_normed * normed, axis=0, keepdims=True)
        )
    ).astype(BF16)
    grad_scores = (dot(grad_ret, values, ((0,), (0,))) * decay * scale).astype(BF16)
    grad_q = dot(keys, grad_scores, ((1,), (1,))).astype(BF16)
    grad_k = dot(query, grad_scores, ((1,), (0,))).astype(BF16)
    grad_v = dot(grad_ret, weights, ((1,), (0,))).astype(BF16)
    grad_qkv = jnp.concatenate(
        [
            grad_q.reshape(depth, -1, seq),
            grad_k.reshape(depth, -1, seq),
            grad_v.reshape(depth, -1, seq),
        ],
        axis=1,
    ).reshape(-1, seq)
    grad_one = group_reduce(
        dot(grad_qkv, all_qkv, ((0,), (0,))) + dot(grad_gate, wt_gate, ((0,), (0,)))
    )

    def from_heads(mine, count):
        send = mine.reshape(2, count, 4, part).transpose(2, 0, 1, 3).reshape(8, count, part)
        return lax.all_to_all(send, GROUP, split_axis=0, concat_axis=0, tiled=True)

    home_go = home(
        jnp.concatenate(
            [
                dot(grad_gate, x_one, ((1,), (0,))).reshape(depth, -1, width),
                grad_out_full.reshape(depth, -1, width),
            ],
            axis=1,
        ).reshape(-1, width)
    )
    home_qkv = home(dot(grad_qkv, x_one, ((1,), (0,))))
    go = from_heads(
        jnp.concatenate(
            [home_go[: 2 * kv].reshape(2, kv, width), home_go[2 * kv :].reshape(2, kv, width)],
            axis=1,
        ),
        2 * kv,
    )
    back = from_heads(
        jnp.concatenate(
            [
                home_qkv[: 2 * kq].reshape(2, kq, width),
                home_qkv[2 * kq : 4 * kq].reshape(2, kq, width),
                home_qkv[4 * kq :].reshape(2, kv, width),
            ],
            axis=1,
        ),
        2 * kq + kv,
    )

    def columns(grads, order):
        return dot(grads.reshape(-1, part), order, ((0,), (1,)))

    out_gate = columns(go[:, :kv], order_v)
    out_out = dot(order_v, go[:, kv:].reshape(-1, part), ((1,), (0,)))
    out_query = columns(back[:, :kq], order_q)
    out_key = columns(back[:, kq : 2 * kq], order_q)
    out_value = columns(back[:, 2 * kq :], order_v)
    back_one, grad_attn_gain, grad_attn_bias = layernorm_back(grad_one, hat_one, inv_one, params[0])
    grad_in = from_tokens((grad_mid + back_one).astype(BF16)).astype(F32)
    totals = lax.psum(
        jnp.stack([grad_attn_gain, grad_attn_bias, grad_ffn_gain, grad_ffn_bias]), EVERY
    )
    totals = lax.dynamic_slice_in_dim(totals, lax.axis_index(ROW) * part, part, 1)
    return (
        block_out,
        grad_in,
        out_query,
        out_key,
        out_value,
        out_gate,
        out_out,
        grad_up,
        grad_down,
        totals[0],
        totals[1],
        totals[2],
        totals[3],
    )


def solution(mesh):
    rows, cols = mesh.devices.shape
    fine = Mesh(mesh.devices.reshape(rows // 2, 2, cols // 2, 2), ("x", "k", "z", "y"))
    row, col = (("x", "k"), ("z", "y"))
    tok, unit = (P(col, row), P(row, col))
    return jax.shard_map(
        body,
        mesh=fine,
        in_specs=(tok, tok, P(row), unit, unit, unit, unit, tok, unit, tok) + (P(row),) * 4,
        out_specs=(tok, tok, unit, unit, unit, unit, tok, unit, tok) + (P(row),) * 4,
        check_vma=False,
    )
```

profile of v0, /device:TPU:0, one launch (start us, length us, event | category | flops | bytes accessed | tf_op | source)
XLA Modules:
  0.0 720.1 jit_solution(10810222214048122269)
XLA Ops:
  10.6 19.4 %all_to_all.60 = bf16[8,128,512]{2,1,0:T(8,128)(2,1)S(1)} all-to-all(bf16[8,128,512]{2,1,0:T(8,128)(2,1)S(1)} %pad_maximum_fusion.10), channel_id=1, replica_groups=mesh['x'=2,'k'=2,'z'=4,'y'=2] {'x','k','y'}, dimensions={0} | all-to-all | bytes 2097152 | tf_op jit(solution)/shard_map/all_to_all | solution.py:129
  34.4 17.0 %all_to_all.61 = bf16[8,128,512]{2,1,0:T(8,128)(2,1)S(1)} all-to-all(bf16[8,128,512]{2,1,0:T(8,128)(2,1)S(1)} %pad_maximum_fusion.12), channel_id=1, replica_groups=mesh['x'=2,'k'=2,'z'=4,'y'=2] {'x','k','y'}, dimensions={0} | all-to-all | bytes 2097152 | tf_op jit(solution)/shard_map/all_to_all | solution.py:129
  59.7 9.8 %all_gather.19 = f32[4,2048]{1,0:T(4,128)S(1)} all-gather(f32[4,512]{1,0:T(4,128)S(1)} %pad_maximum_fusion.16), channel_id=1, replica_groups=mesh['x'=2,'k'=2,'z'=4,'y'=2] {'x','k'}, dimensions={1}, use_global_device_ids=true | all-gather | bytes 40960 | tf_op jit(solution)/shard_map/all_gather | solution.py:163
  76.5 10.8 %collective-permute-done.2 = bf16[128,2048]{1,0:T(8,128)(2,1)} collective-permute-done((bf16[128,2048]{1,0:T(8,128)(2,1)}, bf16[128,2048]{1,0:T(8,128)(2,1)}, u32[]{:S(2)}, u32[]{:S(2)}) %collective-permute-start.2) | collective-permute-done | bytes 524320 | tf_op jit(solution)/shard_map/ppermute | solution.py:22
  87.4 10.6 %collective-permute-done.1 = bf16[128,2048]{1,0:T(8,128)(2,1)} collective-permute-done((bf16[128,2048]{1,0:T(8,128)(2,1)}, bf16[128,2048]{1,0:T(8,128)(2,1)}, u32[]{:S(2)}, u32[]{:S(2)}) %collective-permute-start.1) | collective-permute-done | bytes 524320 | tf_op jit(solution)/shard_map/ppermute | solution.py:22
  99.8 5.7 all_gather.21
  114.1 4.7 fusion.117
  118.8 76.7 %all-gather.7.cloned.1.call-done = bf16[1024,2048]{1,0:T(8,128)(2,1)} async-done(((bf16[256,2048]{1,0:T(8,128)(2,1)}), bf16[1024,2048]{1,0:T(8,128)(2,1)}) %all-gather.7.cloned.1.call-update) | async-done | bytes 4194320 | tf_op jit(solution)/shard_map/all_gather | solution.py:155
  195.5 8.0 %convolution_convert_fusion.5 = bf16[1024,1024]{1,0:T(8,128)(2,1)S(1)} fusion(bf16[1024,2048]{1,0:T(8,128)(2,1)} %all-gather.7.cloned.1.call-done, bf16[1024,2048]{1,0:T(8,128)(2,1)} %bitcast.420), kind=kOutput, calls=%fused_computation.105 | convolution fusion | flops 4296015872 | bytes 10485760 | tf_op jit(solution)/shard_map/dot_general | solution.py:18
  249.4 20.6 %all-to-all-done.3 = bf16[4,128,512]{2,1,0:T(8,128)(2,1)S(1)} async-done(((bf16[4,128,512]{2,1,0:T(8,128)(2,1)}), bf16[4,128,512]{2,1,0:T(8,128)(2,1)S(1)}, u32[]{:S(2)}, u32[]{:S(2)}) %all-to-all-start.3) | async-done | bytes 524320 | tf_op jit(solution)/shard_map/all_to_all | solution.py:41
  277.5 4.9 collective-permute-done.18
  283.8 8.8 %collective-permute-done.17 = bf16[128,2048]{1,0:T(8,128)(2,1)} collective-permute-done((bf16[128,2048]{1,0:T(8,128)(2,1)S(1)}, bf16[128,2048]{1,0:T(8,128)(2,1)}, u32[]{:S(2)}, u32[]{:S(2)}) %collective-permute-start.17) | collective-permute-done | bytes 524320 | tf_op jit(solution)/shard_map/ppermute | solution.py:22
  295.6 8.1 %collective-permute-done.9 = bf16[128,2048]{1,0:T(8,128)(2,1)S(1)} collective-permute-done((bf16[128,2048]{1,0:T(8,128)(2,1)S(1)}, bf16[128,2048]{1,0:T(8,128)(2,1)S(1)}, u32[]{:S(2)}, u32[]{:S(2)}) %collective-permute-start.9) | collective-permute-done | bytes 524320 | tf_op jit(solution)/shard_map/ppermute | solution.py:22
  304.6 10.2 %collective-permute-done.10 = bf16[128,2048]{1,0:T(8,128)(2,1)S(1)} collective-permute-done((bf16[128,2048]{1,0:T(8,128)(2,1)S(1)}, bf16[128,2048]{1,0:T(8,128)(2,1)S(1)}, u32[]{:S(2)}, u32[]{:S(2)}) %collective-permute-start.10) | collective-permute-done | bytes 524320 | tf_op jit(solution)/shard_map/ppermute | solution.py:22
  316.5 11.5 %all_to_all.62 = bf16[4,128,512]{2,1,0:T(8,128)(2,1)S(1)} all-to-all(bf16[4,128,512]{2,1,0:T(8,128)(2,1)S(1)} %bitcast.472), channel_id=1, replica_groups=mesh['x'=2,'k'=2,'z'=4,'y'=2] {'x','k'}, dimensions={0} | all-to-all | bytes 1048576 | tf_op jit(solution)/shard_map/all_to_all | solution.py:41
  329.1 4.7 pad_maximum_fusion.2
  338.5 10.6 %fusion.40 = (bf16[512,1024]{1,0:T(8,128)(2,1)}, f32[512,1024]{1,0:T(8,128)}, f32[1024,512]{0,1:T(8,128)}) fusion(bf16[1024,2048]{1,0:T(8,128)(2,1)} %bitcast.427, bf16[512,2048]{0,1:T(8,128)(2,1)} %all-gather.9.cloned.1.call-done), kind=kOutput, calls=%fused_computation.81 | convolution fusion | flops 2181562368 | bytes 11534336 | tf_op jit(solution)/shard_map/dot_general | solution.py:18
  349.0 23.0 %all-gather.11.cloned.1.call-done = bf16[512,2048]{0,1:T(8,128)(2,1)} async-done(((bf16[128,2048]{0,1:T(8,128)(2,1)}), bf16[512,2048]{0,1:T(8,128)(2,1)}) %all-gather.11.cloned.1.call-update) | async-done | bytes 2097168 | tf_op jit(solution)/shard_map/all_gather | solution.py:155
  372.1 7.1 fusion.37
  411.9 17.0 %collective-permute-done.21 = bf16[128,2048]{1,0:T(8,128)(2,1)S(1)} collective-permute-done((bf16[128,2048]{1,0:T(8,128)(2,1)S(1)}, bf16[128,2048]{1,0:T(8,128)(2,1)S(1)}, u32[]{:S(2)}, u32[]{:S(2)}) %collective-permute-start.21) | collective-permute-done | bytes 524320 | tf_op jit(solution)/shard_map/ppermute | solution.py:22
  431.2 19.1 %collective-permute-done.13 = bf16[128,2048]{1,0:T(8,128)(2,1)S(1)} collective-permute-done((bf16[128,2048]{1,0:T(8,128)(2,1)S(1)}, bf16[128,2048]{1,0:T(8,128)(2,1)S(1)}, u32[]{:S(2)}, u32[]{:S(2)}) %collective-permute-start.13) | collective-permute-done | bytes 524320 | tf_op jit(solution)/shard_map/ppermute | solution.py:22
  457.1 12.3 %collective-permute-done.26 = bf16[128,2048]{1,0:T(8,128)(2,1)S(1)} collective-permute-done((bf16[128,2048]{1,0:T(8,128)(2,1)S(1)}, bf16[128,2048]{1,0:T(8,128)(2,1)S(1)}, u32[]{:S(2)}, u32[]{:S(2)}) %collective-permute-start.26) | collective-permute-done | bytes 524320 | tf_op jit(solution)/shard_map/ppermute | solution.py:22
  469.4 9.3 %collective-permute-done.25 = bf16[128,2048]{1,0:T(8,128)(2,1)S(1)} collective-permute-done((bf16[128,2048]{1,0:T(8,128)(2,1)S(1)}, bf16[128,2048]{1,0:T(8,128)(2,1)S(1)}, u32[]{:S(2)}, u32[]{:S(2)}) %collective-permute-start.25) | collective-permute-done | bytes 524320 | tf_op jit(solution)/shard_map/ppermute | solution.py:22
  512.3 6.0 convolution_convert_fusion
  518.4 7.3 %fusion.131 = f32[1024,2048]{1,0:T(8,128)S(1)} fusion(bf16[1024,1024]{1,0:T(8,128)(2,1)} %bitcast.444, bf16[1024,2048]{1,0:T(8,128)(2,1)} %all-gather.7.cloned.1.call-done), kind=kOutput, calls=%fused_computation.267 | convolution fusion | flops 4294967296 | bytes 14680064 | tf_op jit(solution)/shard_map/dot_general | solution.py:18
  537.6 8.9 %all-to-all-done.5 = bf16[4,128,512]{2,1,0:T(8,128)(2,1)} async-done(((bf16[4,128,512]{2,1,0:T(8,128)(2,1)}), bf16[4,128,512]{2,1,0:T(8,128)(2,1)}, u32[]{:S(2)}, u32[]{:S(2)}) %all-to-all-start.5) | async-done | bytes 524320 | tf_op jit(solution)/shard_map/all_to_all | solution.py:41
  558.0 5.4 all-to-all-done.10
  579.2 15.4 %collective-permute-done.29 = bf16[128,2048]{1,0:T(8,128)(2,1)} collective-permute-done((bf16[128,2048]{1,0:T(8,128)(2,1)}, bf16[128,2048]{1,0:T(8,128)(2,1)}, u32[]{:S(2)}, u32[]{:S(2)}) %collective-permute-start.29) | collective-permute-done | bytes 524320 | tf_op jit(solution)/shard_map/ppermute | solution.py:22
  610.1 4.9 all-to-all-done.7
  618.5 48.9 %psum.7 = f32[4,2048]{1,0:T(4,128)S(1)} all-reduce(f32[4,2048]{1,0:T(4,128)S(1)} %pad_maximum_fusion.15), channel_id=1, replica_groups=mesh['x'=2,'k'=2,'z'=4,'y'=2] {'x','k','z','y'}, use_global_device_ids=true, to_apply=%region_22.23 | all-reduce | flops 8192 | bytes 65536 | tf_op jit(solution)/shard_map/psum | solution.py:299
  668.1 17.8 %reduce-scatter.5.cloned.1.call-done = bf16[256,2048]{1,0:T(8,128)(2,1)} async-done(((bf16[1024,2048]{1,0:T(8,128)(2,1)}), bf16[256,2048]{1,0:T(8,128)(2,1)}) %reduce-scatter.5.cloned.1.call-update) | async-done | bytes 1048592 | tf_op jit(solution)/shard_map/reduce_scatter | solution.py:217
  697.0 10.3 %all-to-all-done.8 = bf16[8,128,512]{2,1,0:T(8,128)(2,1)S(1)} async-done(((bf16[8,128,512]{2,1,0:T(8,128)(2,1)}), bf16[8,128,512]{2,1,0:T(8,128)(2,1)S(1)}, u32[]{:S(2)}, u32[]{:S(2)}) %all-to-all-start.8) | async-done | bytes 1048608 | tf_op jit(solution)/shard_map/all_to_all | solution.py:258
  (345 shorter events, 249.6 us)
Async XLA Ops:
  7.2 106.9 %all-gather.5.cloned.1.call-start = ((), (), s32[]{:S(2)}) async-start(), calls=%async_computation.16 | async-start | bytes 5242880 | tf_op jit(solution)/shard_map/all_gather | solution.py:155
  32.9 162.7 %all-gather.7.cloned.1.call-start = ((), (), s32[]{:S(2)}) async-start(), calls=%async_computation.17 | async-start | bytes 5242880 | tf_op jit(solution)/shard_map/all_gather | solution.py:155
  72.6 25.4 %collective-permute-start.1 = (bf16[128,2048]{1,0:T(8,128)(2,1)}, bf16[128,2048]{1,0:T(8,128)(2,1)}, u32[]{:S(2)}, u32[]{:S(2)}) collective-permute-start(bf16[128,2048]{1,0:T(8,128)(2,1)} %add_convert_fusion.2), channel_id=1, source_target_pairs={{0,16},{1,17},{8,24},{9,25},{16,0},{17,1},{24,8},{25,9},{2,18},{3,... | collective-permute-start | bytes 1572872 | tf_op jit(solution)/shard_map/ppermute | solution.py:22
  74.3 23.7 %collective-permute-start = (bf16[128,2048]{1,0:T(8,128)(2,1)}, bf16[128,2048]{1,0:T(8,128)(2,1)}, u32[]{:S(2)}, u32[]{:S(2)}) collective-permute-start(bf16[128,2048]{1,0:T(8,128)(2,1)} %add_convert_fusion.2), channel_id=1, source_target_pairs={{0,1},{1,0},{8,9},{9,8},{16,17},{17,16},{24,25},{25,24},{2,3},{3,2... | collective-permute-start | bytes 1572872 | tf_op jit(solution)/shard_map/ppermute | solution.py:22
  236.6 34.6 %collective-permute-start.5 = (bf16[128,2048]{1,0:T(8,128)(2,1)}, bf16[128,2048]{1,0:T(8,128)(2,1)}, u32[]{:S(2)}, u32[]{:S(2)}) collective-permute-start(bf16[128,2048]{1,0:T(8,128)(2,1)} %get-tuple-element.48), channel_id=1, source_target_pairs={{0,1},{1,0},{8,9},{9,8},{16,17},{17,16},{24,25},{25,24},{2,3},{3,2... | collective-permute-start | bytes 1572872 | tf_op jit(solution)/shard_map/ppermute | solution.py:22
  238.2 34.7 %collective-permute-start.7 = (bf16[128,2048]{1,0:T(8,128)(2,1)}, bf16[128,2048]{1,0:T(8,128)(2,1)}, u32[]{:S(2)}, u32[]{:S(2)}) collective-permute-start(bf16[128,2048]{1,0:T(8,128)(2,1)} %get-tuple-element.49), channel_id=1, source_target_pairs={{0,17},{1,16},{8,25},{9,24},{16,1},{17,0},{24,9},{25,8},{2,19},{3,... | collective-permute-start | bytes 1572872 | tf_op jit(solution)/shard_map/ppermute | solution.py:22
  239.7 33.2 %collective-permute-start.6 = (bf16[128,2048]{1,0:T(8,128)(2,1)}, bf16[128,2048]{1,0:T(8,128)(2,1)}, u32[]{:S(2)}, u32[]{:S(2)}) collective-permute-start(bf16[128,2048]{1,0:T(8,128)(2,1)} %get-tuple-element.50), channel_id=1, source_target_pairs={{0,16},{1,17},{8,24},{9,25},{16,0},{17,1},{24,8},{25,9},{2,18},{3,... | collective-permute-start | bytes 1572872 | tf_op jit(solution)/shard_map/ppermute | solution.py:22
  241.1 28.8 %all-to-all-start.3 = ((bf16[4,128,512]{2,1,0:T(8,128)(2,1)}), bf16[4,128,512]{2,1,0:T(8,128)(2,1)S(1)}, u32[]{:S(2)}, u32[]{:S(2)}) async-start(bf16[4,128,512]{2,1,0:T(8,128)(2,1)} %bitcast.60), calls=%async_computation.3 | async-start | bytes 1048576 | tf_op jit(solution)/shard_map/all_to_all | solution.py:41
  244.6 93.8 %all-gather.9.cloned.1.call-start = ((), (), s32[]{:S(2)}) async-start(), calls=%async_computation.18 | async-start | bytes 2621440 | tf_op jit(solution)/shard_map/all_gather | solution.py:155
  244.7 37.6 %collective-permute-start.18 = (bf16[128,2048]{1,0:T(8,128)(2,1)S(1)}, bf16[128,2048]{1,0:T(8,128)(2,1)}, u32[]{:S(2)}, u32[]{:S(2)}) collective-permute-start(bf16[128,2048]{1,0:T(8,128)(2,1)S(1)} %bitcast.434), channel_id=1, source_target_pairs={{0,17},{1,16},{8,25},{9,24},{16,1},{17,0},{24,9},{25,8},{2,19},{3,... | collective-permute-start | bytes 1572872 | tf_op jit(solution)/shard_map/ppermute | solution.py:22
  247.7 44.9 %collective-permute-start.17 = (bf16[128,2048]{1,0:T(8,128)(2,1)S(1)}, bf16[128,2048]{1,0:T(8,128)(2,1)}, u32[]{:S(2)}, u32[]{:S(2)}) collective-permute-start(bf16[128,2048]{1,0:T(8,128)(2,1)S(1)} %bitcast.435), channel_id=1, source_target_pairs={{0,16},{1,17},{8,24},{9,25},{16,0},{17,1},{24,8},{25,9},{2,18},{3,... | collective-permute-start | bytes 1572872 | tf_op jit(solution)/shard_map/ppermute | solution.py:22
  271.0 101.1 %all-gather.11.cloned.1.call-start = ((), (), s32[]{:S(2)}) async-start(), calls=%async_computation.19 | async-start | bytes 2621440 | tf_op jit(solution)/shard_map/all_gather | solution.py:155
  275.4 28.3 %collective-permute-start.9 = (bf16[128,2048]{1,0:T(8,128)(2,1)S(1)}, bf16[128,2048]{1,0:T(8,128)(2,1)S(1)}, u32[]{:S(2)}, u32[]{:S(2)}) collective-permute-start(bf16[128,2048]{1,0:T(8,128)(2,1)S(1)} %add_convert_fusion.1), channel_id=1, source_target_pairs={{0,16},{1,17},{8,24},{9,25},{16,0},{17,1},{24,8},{25,9},{2,18},{3,... | collective-permute-start | bytes 1572872 | tf_op jit(solution)/shard_map/ppermute | solution.py:22
  276.9 27.7 %collective-permute-start.8 = (bf16[128,2048]{1,0:T(8,128)(2,1)S(1)}, bf16[128,2048]{1,0:T(8,128)(2,1)S(1)}, u32[]{:S(2)}, u32[]{:S(2)}) collective-permute-start(bf16[128,2048]{1,0:T(8,128)(2,1)S(1)} %add_convert_fusion.1), channel_id=1, source_target_pairs={{0,1},{1,0},{8,9},{9,8},{16,17},{17,16},{24,25},{25,24},{2,3},{3,2... | collective-permute-start | bytes 1572872 | tf_op jit(solution)/shard_map/ppermute | solution.py:22
  282.3 32.5 %collective-permute-start.10 = (bf16[128,2048]{1,0:T(8,128)(2,1)S(1)}, bf16[128,2048]{1,0:T(8,128)(2,1)S(1)}, u32[]{:S(2)}, u32[]{:S(2)}) collective-permute-start(bf16[128,2048]{1,0:T(8,128)(2,1)S(1)} %add_convert_fusion.1), channel_id=1, source_target_pairs={{0,17},{1,16},{8,25},{9,24},{16,1},{17,0},{24,9},{25,8},{2,19},{3,... | collective-permute-start | bytes 1572872 | tf_op jit(solution)/shard_map/ppermute | solution.py:22
  295.4 33.7 %collective-permute-start.19 = (bf16[2,1,2,128,2048]{4,3,2,1,0:T(8,128)(2,1)}, bf16[2,1,2,128,2048]{4,3,2,1,0:T(8,128)(2,1)}, u32[]{:S(2)}, u32[]{:S(2)}) collective-permute-start(bf16[2,1,2,128,2048]{4,3,2,1,0:T(8,128)(2,1)} %bitcast.83), channel_id=1, source_target_pairs={{0,8},{1,9},{8,0},{9,1},{16,24},{17,25},{24,16},{25,17},{2,10},{3,... | collective-permute-start | bytes 6291464 | tf_op jit(solution)/shard_map/ppermute | solution.py:22
  329.0 217.4 %reduce-scatter.9.cloned.1.call-start = ((), (), s32[]{:S(2)}) async-start(), calls=%async_computation.22 | async-start | bytes 2621440 | tf_op jit(solution)/shard_map/reduce_scatter | solution.py:217
  398.5 149.8 %reduce-scatter.11.cloned.1.call-start = ((), (), s32[]{:S(2)}) async-start(), calls=%async_computation.23 | async-start | bytes 2621440 | tf_op jit(solution)/shard_map/reduce_scatter | solution.py:217
  402.9 26.1 %collective-permute-start.21 = (bf16[128,2048]{1,0:T(8,128)(2,1)S(1)}, bf16[128,2048]{1,0:T(8,128)(2,1)S(1)}, u32[]{:S(2)}, u32[]{:S(2)}) collective-permute-start(bf16[128,2048]{1,0:T(8,128)(2,1)S(1)} %get-tuple-element.42), channel_id=1, source_target_pairs={{0,1},{1,0},{8,9},{9,8},{16,17},{17,16},{24,25},{25,24},{2,3},{3,2... | collective-permute-start | bytes 1572872 | tf_op jit(solution)/shard_map/ppermute | solution.py:22
  404.4 26.0 %collective-permute-start.23 = (bf16[128,2048]{1,0:T(8,128)(2,1)S(1)}, bf16[128,2048]{1,0:T(8,128)(2,1)S(1)}, u32[]{:S(2)}, u32[]{:S(2)}) collective-permute-start(bf16[128,2048]{1,0:T(8,128)(2,1)S(1)} %get-tuple-element.43), channel_id=1, source_target_pairs={{0,17},{1,16},{8,25},{9,24},{16,1},{17,0},{24,9},{25,8},{2,19},{3,... | collective-permute-start | bytes 1572872 | tf_op jit(solution)/shard_map/ppermute | solution.py:22
  405.9 24.6 %collective-permute-start.22 = (bf16[128,2048]{1,0:T(8,128)(2,1)S(1)}, bf16[128,2048]{1,0:T(8,128)(2,1)S(1)}, u32[]{:S(2)}, u32[]{:S(2)}) collective-permute-start(bf16[128,2048]{1,0:T(8,128)(2,1)S(1)} %get-tuple-element.44), channel_id=1, source_target_pairs={{0,16},{1,17},{8,24},{9,25},{16,0},{17,1},{24,8},{25,9},{2,18},{3,... | collective-permute-start | bytes 1572872 | tf_op jit(solution)/shard_map/ppermute | solution.py:22
  408.9 41.4 %collective-permute-start.13 = (bf16[128,2048]{1,0:T(8,128)(2,1)S(1)}, bf16[128,2048]{1,0:T(8,128)(2,1)S(1)}, u32[]{:S(2)}, u32[]{:S(2)}) collective-permute-start(bf16[128,2048]{1,0:T(8,128)(2,1)S(1)} %get-tuple-element.45), channel_id=1, source_target_pairs={{0,1},{1,0},{8,9},{9,8},{16,17},{17,16},{24,25},{25,24},{2,3},{3,2... | collective-permute-start | bytes 1572872 | tf_op jit(solution)/shard_map/ppermute | solution.py:22
  410.5 39.8 %collective-permute-start.15 = (bf16[128,2048]{1,0:T(8,128)(2,1)S(1)}, bf16[128,2048]{1,0:T(8,128)(2,1)S(1)}, u32[]{:S(2)}, u32[]{:S(2)}) collective-permute-start(bf16[128,2048]{1,0:T(8,128)(2,1)S(1)} %get-tuple-element.46), channel_id=1, source_target_pairs={{0,17},{1,16},{8,25},{9,24},{16,1},{17,0},{24,9},{25,8},{2,19},{3,... | collective-permute-start | bytes 1572872 | tf_op jit(solution)/shard_map/ppermute | solution.py:22
  429.0 22.7 %collective-permute-start.14 = (bf16[128,2048]{1,0:T(8,128)(2,1)S(1)}, bf16[128,2048]{1,0:T(8,128)(2,1)S(1)}, u32[]{:S(2)}, u32[]{:S(2)}) collective-permute-start(bf16[128,2048]{1,0:T(8,128)(2,1)S(1)} %get-tuple-element.47), channel_id=1, source_target_pairs={{0,16},{1,17},{8,24},{9,25},{16,0},{17,1},{24,8},{25,9},{2,18},{3,... | collective-permute-start | bytes 1572872 | tf_op jit(solution)/shard_map/ppermute | solution.py:22
  456.1 22.6 %collective-permute-start.25 = (bf16[128,2048]{1,0:T(8,128)(2,1)S(1)}, bf16[128,2048]{1,0:T(8,128)(2,1)S(1)}, u32[]{:S(2)}, u32[]{:S(2)}) collective-permute-start(bf16[128,2048]{1,0:T(8,128)(2,1)S(1)} %get-tuple-element.27), channel_id=1, source_target_pairs={{0,16},{1,17},{8,24},{9,25},{16,0},{17,1},{24,8},{25,9},{2,18},{3,... | collective-permute-start | bytes 1572872 | tf_op jit(solution)/shard_map/ppermute | solution.py:22
  484.6 121.5 %reduce-scatter.7.cloned.1.call-start = ((), (), s32[]{:S(2)}) async-start(), calls=%async_computation.21 | async-start | bytes 5242880 | tf_op jit(solution)/shard_map/reduce_scatter | solution.py:217
  499.5 186.3 %reduce-scatter.5.cloned.1.call-start = ((), (), s32[]{:S(2)}) async-start(), calls=%async_computation.20 | async-start | bytes 5242880 | tf_op jit(solution)/shard_map/reduce_scatter | solution.py:217
  531.9 22.5 %collective-permute-start.28 = (bf16[2,2,128,2048]{3,2,1,0:T(8,128)(2,1)S(1)}, bf16[2,2,128,2048]{3,2,1,0:T(8,128)(2,1)}, u32[]{:S(2)}, u32[]{:S(2)}) collective-permute-start(bf16[2,2,128,2048]{3,2,1,0:T(8,128)(2,1)S(1)} %fusion.31), channel_id=1, source_target_pairs={{0,8},{1,9},{8,0},{9,1},{16,24},{17,25},{24,16},{25,17},{2,10},{3,... | collective-permute-start | bytes 6291464 | tf_op jit(solution)/shard_map/ppermute | solution.py:22
  568.8 25.8 %collective-permute-start.29 = (bf16[128,2048]{1,0:T(8,128)(2,1)}, bf16[128,2048]{1,0:T(8,128)(2,1)}, u32[]{:S(2)}, u32[]{:S(2)}) collective-permute-start(bf16[128,2048]{1,0:T(8,128)(2,1)} %get-tuple-element.37), channel_id=1, source_target_pairs={{0,1},{1,0},{8,9},{9,8},{16,17},{17,16},{24,25},{25,24},{2,3},{3,2... | collective-permute-start | bytes 1572872 | tf_op jit(solution)/shard_map/ppermute | solution.py:22
  570.3 24.4 %collective-permute-start.31 = (bf16[128,2048]{1,0:T(8,128)(2,1)}, bf16[128,2048]{1,0:T(8,128)(2,1)}, u32[]{:S(2)}, u32[]{:S(2)}) collective-permute-start(bf16[128,2048]{1,0:T(8,128)(2,1)} %get-tuple-element.38), channel_id=1, source_target_pairs={{0,17},{1,16},{8,25},{9,24},{16,1},{17,0},{24,9},{25,8},{2,19},{3,... | collective-permute-start | bytes 1572872 | tf_op jit(solution)/shard_map/ppermute | solution.py:22
  572.3 26.8 %collective-permute-start.30 = (bf16[128,2048]{1,0:T(8,128)(2,1)}, bf16[128,2048]{1,0:T(8,128)(2,1)}, u32[]{:S(2)}, u32[]{:S(2)}) collective-permute-start(bf16[128,2048]{1,0:T(8,128)(2,1)} %get-tuple-element.39), channel_id=1, source_target_pairs={{0,16},{1,17},{8,24},{9,25},{16,0},{17,1},{24,8},{25,9},{2,18},{3,... | collective-permute-start | bytes 1572872 | tf_op jit(solution)/shard_map/ppermute | solution.py:22
  614.9 74.1 %all-to-all-start.9 = ((bf16[8,128,512]{2,1,0:T(8,128)(2,1)}), bf16[8,128,512]{2,1,0:T(8,128)(2,1)S(1)}, u32[]{:S(2)}, u32[]{:S(2)}) async-start(bf16[8,128,512]{2,1,0:T(8,128)(2,1)} %bitcast.126), calls=%async_computation.11 | async-start | bytes 2097152 | tf_op jit(solution)/shard_map/all_to_all | solution.py:258
  (76 other events, 578.7 us)
Sparse Core Ops, SparseCore 0:
  33.0 81.0 all-gather.4
  116.2 79.2 all-gather.6
  271.1 44.7 all-gather.8
  329.2 42.8 all-gather.10
  398.7 42.0 reduce-scatter.8
  484.7 41.9 reduce-scatter.10
  529.0 76.0 reduce-scatter.6
  607.5 78.3 reduce-scatter.4
where the time goes:
time: 729 us; the launch traced here: 720 us
  waiting for transfers between devices  306 us (42%)
  blocking collectives  112 us (15%)
  matrix products  89.1 us (12%)
  local copies, waits for them, and re-layouts  75 us (10%)
  starting transfers between devices  65.3 us (9%)
  other arithmetic  56.8 us (8%)
  between operations  15.7 us (2%)
    ppermute x32, waiting for transfers between devices, swap(): return lax.ppermute(value, GROUP, [(i, i ^ mask) for i in range(8)])  134 us
    all_gather x4, waiting for transfers between devices, planes(): return lax.all_gather(mine, 'z', axis=0, tiled=True)  104 us
    dot_general x31, matrix products, dot(): lax.dot_general(left, right, (over, ((), ())), preferred_element_type=F32)  89.1 us
    psum x1, blocking collectives, body(): lax.psum(jnp.stack([grad_attn_gain, grad_attn_bias, grad_ffn_gain, grad_f...  48.9 us
    all_to_all x7, waiting for transfers between devices, row_exchange(): return lax.all_to_all(parts, ROW, split_axis=0, concat_axis=0, tiled=True)  39.7 us
    all_to_all x2, blocking collectives, to_heads(): got = lax.all_to_all(send, GROUP, split_axis=0, concat_axis=0, tiled=True)  36.4 us
    unnamed x118, local copies, waits for them, and re-layouts  33.2 us
    ppermute x32, starting transfers between devices, swap(): return lax.ppermute(value, GROUP, [(i, i ^ mask) for i in range(8)])  30.5 us
  transfers between devices with their start and end apart: 49, of which 24 were waited for; matrix products, arithmetic and copies ran while one was open for 20% of the time, Pallas kernels for 0%

commit v1 on v0

--- a/solution.py
+++ b/solution.py
@@ -296,8 +296,11 @@
     out_value = columns(back[:, 2 * kq :], order_v)
     back_one, grad_attn_gain, grad_attn_bias = layernorm_back(grad_one, hat_one, inv_one, params[0])
     grad_in = from_tokens((grad_mid + back_one).astype(BF16)).astype(F32)
-    totals = lax.psum(
-        jnp.stack([grad_attn_gain, grad_attn_bias, grad_ffn_gain, grad_ffn_bias]), EVERY
+    totals = jnp.sum(
+        lax.all_gather(
+            jnp.stack([grad_attn_gain, grad_attn_bias, grad_ffn_gain, grad_ffn_bias]), EVERY
+        ),
+        axis=0,
     )
     totals = lax.dynamic_slice_in_dim(totals, lax.axis_index(ROW) * part, part, 1)
     return (

time: 729 us -> 771 us (1.058)
  waiting for transfers between devices: 306 us -> 404 us
  blocking collectives: 112 us -> 63.4 us
    reduce_scatter x4, waiting for transfers between devices: 17.8 us -> 73.9 us  [home(): lax.psum_scatter(full.astype(BF16), 'z', scatter_dimension=0, tiled=True)]
    all_gather x0 -> x1, waiting for transfers between devices: none -> 52.2 us  [body(): lax.all_gather(jnp.stack([grad_attn_gain, grad_attn_bias, grad_ffn_gain,...]
    psum x1 -> x0, blocking collectives: 48.9 us -> none  [body(): lax.psum(jnp.stack([grad_attn_gain, grad_attn_bias, grad_ffn_gain, grad_f...]
    ppermute x32, waiting for transfers between devices: 134 us -> 119 us  [swap(): return lax.ppermute(value, GROUP, [(i, i ^ mask) for i in range(8)])]
    all_to_all x7, waiting for transfers between devices: 39.7 us -> 55.4 us  [row_exchange(): return lax.all_to_all(parts, ROW, split_axis=0, concat_axis=0, tiled=True)]
    all_to_all x2, waiting for transfers between devices: 10.3 us -> 0.01 us  [from_heads(): return lax.all_to_all(send, GROUP, split_axis=0, concat_axis=0, tiled=True)]
    unnamed x118 -> x114, local copies, waits for them, and re-layouts: 33.2 us -> 29.2 us
  transfers between devices with their start and end apart: 49 -> 50, of which waited for: 24 -> 24; matrix products, arithmetic and copies ran while one was open for 20% -> 19% of each run, Pallas kernels for 0% -> 0%
where the time goes in v1:
time: 771 us; the launch traced here: 763 us
  waiting for transfers between devices  404 us (52%)
  matrix products  89.2 us (12%)
  local copies, waits for them, and re-layouts  69.7 us (9%)
  starting transfers between devices  65 us (8%)
  blocking collectives  63.4 us (8%)
  other arithmetic  56.2 us (7%)
  between operations  15.5 us (2%)
    ppermute x32, waiting for transfers between devices, swap(): return lax.ppermute(value, GROUP, [(i, i ^ mask) for i in range(8)])  119 us
    all_gather x4, waiting for transfers between devices, planes(): return lax.all_gather(mine, 'z', axis=0, tiled=True)  104 us
    dot_general x31, matrix products, dot(): lax.dot_general(left, right, (over, ((), ())), preferred_element_type=F32)  89.2 us
    reduce_scatter x4, waiting for transfers between devices, home(): lax.psum_scatter(full.astype(BF16), 'z', scatter_dimension=0, tiled=True)  73.9 us
    all_to_all x7, waiting for transfers between devices, row_exchange(): return lax.all_to_all(parts, ROW, split_axis=0, concat_axis=0, tiled=True)  55.4 us
    all_gather x1, waiting for transfers between devices, body(): lax.all_gather(jnp.stack([grad_attn_gain, grad_attn_bias, grad_ffn_gain,...  52.2 us
    all_to_all x2, blocking collectives, to_heads(): got = lax.all_to_all(send, GROUP, split_axis=0, concat_axis=0, tiled=True)  36.4 us
    ppermute x32, starting transfers between devices, swap(): return lax.ppermute(value, GROUP, [(i, i ^ mask) for i in range(8)])  30.5 us
  transfers between devices with their start and end apart: 50, of which 24 were waited for; matrix products, arithmetic and copies ran while one was open for 19% of the time, Pallas kernels for 0%

profile of v1, /device:TPU:0, one launch (start us, length us, event | category | flops | bytes accessed | tf_op | source)
XLA Modules:
  0.0 762.8 jit_solution(5814087555412238053)
XLA Ops:
  10.6 19.4 %all_to_all.60 = bf16[8,128,512]{2,1,0:T(8,128)(2,1)S(1)} all-to-all(bf16[8,128,512]{2,1,0:T(8,128)(2,1)S(1)} %pad_maximum_fusion.10), channel_id=1, replica_groups=mesh['x'=2,'k'=2,'z'=4,'y'=2] {'x','k','y'}, dimensions={0} | all-to-all | bytes 2097152 | tf_op jit(solution)/shard_map/all_to_all | solution.py:129
  34.4 17.0 %all_to_all.61 = bf16[8,128,512]{2,1,0:T(8,128)(2,1)S(1)} all-to-all(bf16[8,128,512]{2,1,0:T(8,128)(2,1)S(1)} %pad_maximum_fusion.12), channel_id=1, replica_groups=mesh['x'=2,'k'=2,'z'=4,'y'=2] {'x','k','y'}, dimensions={0} | all-to-all | bytes 2097152 | tf_op jit(solution)/shard_map/all_to_all | solution.py:129
  59.7 9.8 %all_gather.25 = f32[4,2048]{1,0:T(4,128)S(1)} all-gather(f32[4,512]{1,0:T(4,128)S(1)} %pad_maximum_fusion.15), channel_id=1, replica_groups=mesh['x'=2,'k'=2,'z'=4,'y'=2] {'x','k'}, dimensions={1}, use_global_device_ids=true | all-gather | bytes 40960 | tf_op jit(solution)/shard_map/all_gather | solution.py:163
  76.5 10.8 %collective-permute-done.2 = bf16[128,2048]{1,0:T(8,128)(2,1)} collective-permute-done((bf16[128,2048]{1,0:T(8,128)(2,1)}, bf16[128,2048]{1,0:T(8,128)(2,1)}, u32[]{:S(2)}, u32[]{:S(2)}) %collective-permute-start.2) | collective-permute-done | bytes 524320 | tf_op jit(solution)/shard_map/ppermute | solution.py:22
  87.4 10.6 %collective-permute-done.1 = bf16[128,2048]{1,0:T(8,128)(2,1)} collective-permute-done((bf16[128,2048]{1,0:T(8,128)(2,1)}, bf16[128,2048]{1,0:T(8,128)(2,1)}, u32[]{:S(2)}, u32[]{:S(2)}) %collective-permute-start.1) | collective-permute-done | bytes 524320 | tf_op jit(solution)/shard_map/ppermute | solution.py:22
  99.8 5.7 all_gather.27
  114.1 4.7 fusion.117
  118.8 76.7 %all-gather.10.cloned.1.call-done = bf16[1024,2048]{1,0:T(8,128)(2,1)} async-done(((bf16[256,2048]{1,0:T(8,128)(2,1)}), bf16[1024,2048]{1,0:T(8,128)(2,1)}) %all-gather.10.cloned.1.call-update) | async-done | bytes 4194320 | tf_op jit(solution)/shard_map/all_gather | solution.py:155
  195.5 8.0 %convolution_convert_fusion.5 = bf16[1024,1024]{1,0:T(8,128)(2,1)S(1)} fusion(bf16[1024,2048]{1,0:T(8,128)(2,1)} %all-gather.10.cloned.1.call-done, bf16[1024,2048]{1,0:T(8,128)(2,1)} %bitcast.422), kind=kOutput, calls=%fused_computation.105 | convolution fusion | flops 4296015872 | bytes 10485760 | tf_op jit(solution)/shard_map/dot_general | solution.py:18
  249.4 20.6 %all-to-all-done.3 = bf16[4,128,512]{2,1,0:T(8,128)(2,1)S(1)} async-done(((bf16[4,128,512]{2,1,0:T(8,128)(2,1)}), bf16[4,128,512]{2,1,0:T(8,128)(2,1)S(1)}, u32[]{:S(2)}, u32[]{:S(2)}) %all-to-all-start.3) | async-done | bytes 524320 | tf_op jit(solution)/shard_map/all_to_all | solution.py:41
  277.5 4.9 collective-permute-done.18
  283.8 8.8 %collective-permute-done.17 = bf16[128,2048]{1,0:T(8,128)(2,1)} collective-permute-done((bf16[128,2048]{1,0:T(8,128)(2,1)S(1)}, bf16[128,2048]{1,0:T(8,128)(2,1)}, u32[]{:S(2)}, u32[]{:S(2)}) %collective-permute-start.17) | collective-permute-done | bytes 524320 | tf_op jit(solution)/shard_map/ppermute | solution.py:22
  295.6 8.1 %collective-permute-done.9 = bf16[128,2048]{1,0:T(8,128)(2,1)S(1)} collective-permute-done((bf16[128,2048]{1,0:T(8,128)(2,1)S(1)}, bf16[128,2048]{1,0:T(8,128)(2,1)S(1)}, u32[]{:S(2)}, u32[]{:S(2)}) %collective-permute-start.9) | collective-permute-done | bytes 524320 | tf_op jit(solution)/shard_map/ppermute | solution.py:22
  304.6 10.2 %collective-permute-done.10 = bf16[128,2048]{1,0:T(8,128)(2,1)S(1)} collective-permute-done((bf16[128,2048]{1,0:T(8,128)(2,1)S(1)}, bf16[128,2048]{1,0:T(8,128)(2,1)S(1)}, u32[]{:S(2)}, u32[]{:S(2)}) %collective-permute-start.10) | collective-permute-done | bytes 524320 | tf_op jit(solution)/shard_map/ppermute | solution.py:22
  316.5 11.5 %all_to_all.62 = bf16[4,128,512]{2,1,0:T(8,128)(2,1)S(1)} all-to-all(bf16[4,128,512]{2,1,0:T(8,128)(2,1)S(1)} %bitcast.474), channel_id=1, replica_groups=mesh['x'=2,'k'=2,'z'=4,'y'=2] {'x','k'}, dimensions={0} | all-to-all | bytes 1048576 | tf_op jit(solution)/shard_map/all_to_all | solution.py:41
  329.1 4.7 pad_maximum_fusion.2
  333.8 4.6 pad_maximum_fusion.1
  338.4 10.6 %fusion.40 = (bf16[512,1024]{1,0:T(8,128)(2,1)}, f32[512,1024]{1,0:T(8,128)}, f32[1024,512]{0,1:T(8,128)}) fusion(bf16[1024,2048]{1,0:T(8,128)(2,1)} %bitcast.429, bf16[512,2048]{0,1:T(8,128)(2,1)} %all-gather.12.cloned.1.call-done), kind=kOutput, calls=%fused_computation.81 | convolution fusion | flops 2181562368 | bytes 11534336 | tf_op jit(solution)/shard_map/dot_general | solution.py:18
  349.0 23.1 %all-gather.14.cloned.1.call-done = bf16[512,2048]{0,1:T(8,128)(2,1)} async-done(((bf16[128,2048]{0,1:T(8,128)(2,1)}), bf16[512,2048]{0,1:T(8,128)(2,1)}) %all-gather.14.cloned.1.call-update) | async-done | bytes 2097168 | tf_op jit(solution)/shard_map/all_gather | solution.py:155
  372.1 7.1 fusion.37
  412.0 17.0 %collective-permute-done.21 = bf16[128,2048]{1,0:T(8,128)(2,1)S(1)} collective-permute-done((bf16[128,2048]{1,0:T(8,128)(2,1)S(1)}, bf16[128,2048]{1,0:T(8,128)(2,1)S(1)}, u32[]{:S(2)}, u32[]{:S(2)}) %collective-permute-start.21) | collective-permute-done | bytes 524320 | tf_op jit(solution)/shard_map/ppermute | solution.py:22
  431.2 19.1 %collective-permute-done.13 = bf16[128,2048]{1,0:T(8,128)(2,1)S(1)} collective-permute-done((bf16[128,2048]{1,0:T(8,128)(2,1)S(1)}, bf16[128,2048]{1,0:T(8,128)(2,1)S(1)}, u32[]{:S(2)}, u32[]{:S(2)}) %collective-permute-start.13) | collective-permute-done | bytes 524320 | tf_op jit(solution)/shard_map/ppermute | solution.py:22
  457.1 12.3 %collective-permute-done.26 = bf16[128,2048]{1,0:T(8,128)(2,1)S(1)} collective-permute-done((bf16[128,2048]{1,0:T(8,128)(2,1)S(1)}, bf16[128,2048]{1,0:T(8,128)(2,1)S(1)}, u32[]{:S(2)}, u32[]{:S(2)}) %collective-permute-start.26) | collective-permute-done | bytes 524320 | tf_op jit(solution)/shard_map/ppermute | solution.py:22
  469.4 9.3 %collective-permute-done.25 = bf16[128,2048]{1,0:T(8,128)(2,1)S(1)} collective-permute-done((bf16[128,2048]{1,0:T(8,128)(2,1)S(1)}, bf16[128,2048]{1,0:T(8,128)(2,1)S(1)}, u32[]{:S(2)}, u32[]{:S(2)}) %collective-permute-start.25) | collective-permute-done | bytes 524320 | tf_op jit(solution)/shard_map/ppermute | solution.py:22
  512.3 6.1 convolution_convert_fusion
  518.4 7.3 fusion.131
  543.4 23.5 %all-to-all-done.5 = bf16[4,128,512]{2,1,0:T(8,128)(2,1)} async-done(((bf16[4,128,512]{2,1,0:T(8,128)(2,1)}), bf16[4,128,512]{2,1,0:T(8,128)(2,1)}, u32[]{:S(2)}, u32[]{:S(2)}) %all-to-all-start.5) | async-done | bytes 524320 | tf_op jit(solution)/shard_map/all_to_all | solution.py:41
  578.5 5.3 all-to-all-done.11
  590.2 5.9 all-to-all-done.10
  599.6 5.6 reduce-scatter.7.cloned.1.call-done
  616.4 68.4 %reduce-scatter.5.cloned.1.call-done = bf16[256,2048]{1,0:T(8,128)(2,1)} async-done(((bf16[1024,2048]{1,0:T(8,128)(2,1)}), bf16[256,2048]{1,0:T(8,128)(2,1)}) %reduce-scatter.5.cloned.1.call-update) | async-done | bytes 1048592 | tf_op jit(solution)/shard_map/reduce_scatter | solution.py:217
  692.8 52.2 %all-gather.16.cloned.1.call-done = f32[32,4,2048]{2,1,0:T(4,128)} async-done(((f32[1,4,2048]{2,1,0:T(4,128)}), f32[32,4,2048]{2,1,0:T(4,128)}) %all-gather.16.cloned.1.call-update) | async-done | bytes 1048592 | tf_op jit(solution)/shard_map/all_gather | solution.py:300
  (344 shorter events, 238.5 us)
Async XLA Ops:
  7.2 106.9 %all-gather.8.cloned.1.call-start = ((), (), s32[]{:S(2)}) async-start(), calls=%async_computation.16 | async-start | bytes 5242880 | tf_op jit(solution)/shard_map/all_gather | solution.py:155
  32.9 162.7 %all-gather.10.cloned.1.call-start = ((), (), s32[]{:S(2)}) async-start(), calls=%async_computation.17 | async-start | bytes 5242880 | tf_op jit(solution)/shard_map/all_gather | solution.py:155
  72.6 25.4 %collective-permute-start.1 = (bf16[128,2048]{1,0:T(8,128)(2,1)}, bf16[128,2048]{1,0:T(8,128)(2,1)}, u32[]{:S(2)}, u32[]{:S(2)}) collective-permute-start(bf16[128,2048]{1,0:T(8,128)(2,1)} %add_convert_fusion.2), channel_id=1, source_target_pairs={{0,16},{1,17},{8,24},{9,25},{16,0},{17,1},{24,8},{25,9},{2,18},{3,... | collective-permute-start | bytes 1572872 | tf_op jit(solution)/shard_map/ppermute | solution.py:22
  74.3 23.7 %collective-permute-start = (bf16[128,2048]{1,0:T(8,128)(2,1)}, bf16[128,2048]{1,0:T(8,128)(2,1)}, u32[]{:S(2)}, u32[]{:S(2)}) collective-permute-start(bf16[128,2048]{1,0:T(8,128)(2,1)} %add_convert_fusion.2), channel_id=1, source_target_pairs={{0,1},{1,0},{8,9},{9,8},{16,17},{17,16},{24,25},{25,24},{2,3},{3,2... | collective-permute-start | bytes 1572872 | tf_op jit(solution)/shard_map/ppermute | solution.py:22
  236.6 34.6 %collective-permute-start.5 = (bf16[128,2048]{1,0:T(8,128)(2,1)}, bf16[128,2048]{1,0:T(8,128)(2,1)}, u32[]{:S(2)}, u32[]{:S(2)}) collective-permute-start(bf16[128,2048]{1,0:T(8,128)(2,1)} %get-tuple-element.48), channel_id=1, source_target_pairs={{0,1},{1,0},{8,9},{9,8},{16,17},{17,16},{24,25},{25,24},{2,3},{3,2... | collective-permute-start | bytes 1572872 | tf_op jit(solution)/shard_map/ppermute | solution.py:22
  238.2 34.7 %collective-permute-start.7 = (bf16[128,2048]{1,0:T(8,128)(2,1)}, bf16[128,2048]{1,0:T(8,128)(2,1)}, u32[]{:S(2)}, u32[]{:S(2)}) collective-permute-start(bf16[128,2048]{1,0:T(8,128)(2,1)} %get-tuple-element.49), channel_id=1, source_target_pairs={{0,17},{1,16},{8,25},{9,24},{16,1},{17,0},{24,9},{25,8},{2,19},{3,... | collective-permute-start | bytes 1572872 | tf_op jit(solution)/shard_map/ppermute | solution.py:22
  239.6 33.2 %collective-permute-start.6 = (bf16[128,2048]{1,0:T(8,128)(2,1)}, bf16[128,2048]{1,0:T(8,128)(2,1)}, u32[]{:S(2)}, u32[]{:S(2)}) collective-permute-start(bf16[128,2048]{1,0:T(8,128)(2,1)} %get-tuple-element.50), channel_id=1, source_target_pairs={{0,16},{1,17},{8,24},{9,25},{16,0},{17,1},{24,8},{25,9},{2,18},{3,... | collective-permute-start | bytes 1572872 | tf_op jit(solution)/shard_map/ppermute | solution.py:22
  241.1 28.8 %all-to-all-start.3 = ((bf16[4,128,512]{2,1,0:T(8,128)(2,1)}), bf16[4,128,512]{2,1,0:T(8,128)(2,1)S(1)}, u32[]{:S(2)}, u32[]{:S(2)}) async-start(bf16[4,128,512]{2,1,0:T(8,128)(2,1)} %bitcast.60), calls=%async_computation.3 | async-start | bytes 1048576 | tf_op jit(solution)/shard_map/all_to_all | solution.py:41
  244.6 93.8 %all-gather.12.cloned.1.call-start = ((), (), s32[]{:S(2)}) async-start(), calls=%async_computation.18 | async-start | bytes 2621440 | tf_op jit(solution)/shard_map/all_gather | solution.py:155
  244.7 37.6 %collective-permute-start.18 = (bf16[128,2048]{1,0:T(8,128)(2,1)S(1)}, bf16[128,2048]{1,0:T(8,128)(2,1)}, u32[]{:S(2)}, u32[]{:S(2)}) collective-permute-start(bf16[128,2048]{1,0:T(8,128)(2,1)S(1)} %bitcast.436), channel_id=1, source_target_pairs={{0,17},{1,16},{8,25},{9,24},{16,1},{17,0},{24,9},{25,8},{2,19},{3,... | collective-permute-start | bytes 1572872 | tf_op jit(solution)/shard_map/ppermute | solution.py:22
  247.7 44.9 %collective-permute-start.17 = (bf16[128,2048]{1,0:T(8,128)(2,1)S(1)}, bf16[128,2048]{1,0:T(8,128)(2,1)}, u32[]{:S(2)}, u32[]{:S(2)}) collective-permute-start(bf16[128,2048]{1,0:T(8,128)(2,1)S(1)} %bitcast.437), channel_id=1, source_target_pairs={{0,16},{1,17},{8,24},{9,25},{16,0},{17,1},{24,8},{25,9},{2,18},{3,... | collective-permute-start | bytes 1572872 | tf_op jit(solution)/shard_map/ppermute | solution.py:22
  271.0 101.1 %all-gather.14.cloned.1.call-start = ((), (), s32[]{:S(2)}) async-start(), calls=%async_computation.19 | async-start | bytes 2621440 | tf_op jit(solution)/shard_map/all_gather | solution.py:155
  275.4 28.3 %collective-permute-start.9 = (bf16[128,2048]{1,0:T(8,128)(2,1)S(1)}, bf16[128,2048]{1,0:T(8,128)(2,1)S(1)}, u32[]{:S(2)}, u32[]{:S(2)}) collective-permute-start(bf16[128,2048]{1,0:T(8,128)(2,1)S(1)} %add_convert_fusion.1), channel_id=1, source_target_pairs={{0,16},{1,17},{8,24},{9,25},{16,0},{17,1},{24,8},{25,9},{2,18},{3,... | collective-permute-start | bytes 1572872 | tf_op jit(solution)/shard_map/ppermute | solution.py:22
  276.9 27.7 %collective-permute-start.8 = (bf16[128,2048]{1,0:T(8,128)(2,1)S(1)}, bf16[128,2048]{1,0:T(8,128)(2,1)S(1)}, u32[]{:S(2)}, u32[]{:S(2)}) collective-permute-start(bf16[128,2048]{1,0:T(8,128)(2,1)S(1)} %add_convert_fusion.1), channel_id=1, source_target_pairs={{0,1},{1,0},{8,9},{9,8},{16,17},{17,16},{24,25},{25,24},{2,3},{3,2... | collective-permute-start | bytes 1572872 | tf_op jit(solution)/shard_map/ppermute | solution.py:22
  282.3 32.5 %collective-permute-start.10 = (bf16[128,2048]{1,0:T(8,128)(2,1)S(1)}, bf16[128,2048]{1,0:T(8,128)(2,1)S(1)}, u32[]{:S(2)}, u32[]{:S(2)}) collective-permute-start(bf16[128,2048]{1,0:T(8,128)(2,1)S(1)} %add_convert_fusion.1), channel_id=1, source_target_pairs={{0,17},{1,16},{8,25},{9,24},{16,1},{17,0},{24,9},{25,8},{2,19},{3,... | collective-permute-start | bytes 1572872 | tf_op jit(solution)/shard_map/ppermute | solution.py:22
  295.4 33.7 %collective-permute-start.19 = (bf16[2,1,2,128,2048]{4,3,2,1,0:T(8,128)(2,1)}, bf16[2,1,2,128,2048]{4,3,2,1,0:T(8,128)(2,1)}, u32[]{:S(2)}, u32[]{:S(2)}) collective-permute-start(bf16[2,1,2,128,2048]{4,3,2,1,0:T(8,128)(2,1)} %bitcast.83), channel_id=1, source_target_pairs={{0,8},{1,9},{8,0},{9,1},{16,24},{17,25},{24,16},{25,17},{2,10},{3,... | collective-permute-start | bytes 6291464 | tf_op jit(solution)/shard_map/ppermute | solution.py:22
  329.0 237.9 %reduce-scatter.9.cloned.1.call-start = ((), (), s32[]{:S(2)}) async-start(), calls=%async_computation.22 | async-start | bytes 2621440 | tf_op jit(solution)/shard_map/reduce_scatter | solution.py:217
  398.5 170.3 %reduce-scatter.11.cloned.1.call-start = ((), (), s32[]{:S(2)}) async-start(), calls=%async_computation.23 | async-start | bytes 2621440 | tf_op jit(solution)/shard_map/reduce_scatter | solution.py:217
  402.9 26.1 %collective-permute-start.21 = (bf16[128,2048]{1,0:T(8,128)(2,1)S(1)}, bf16[128,2048]{1,0:T(8,128)(2,1)S(1)}, u32[]{:S(2)}, u32[]{:S(2)}) collective-permute-start(bf16[128,2048]{1,0:T(8,128)(2,1)S(1)} %get-tuple-element.42), channel_id=1, source_target_pairs={{0,1},{1,0},{8,9},{9,8},{16,17},{17,16},{24,25},{25,24},{2,3},{3,2... | collective-permute-start | bytes 1572872 | tf_op jit(solution)/shard_map/ppermute | solution.py:22
  404.4 26.0 %collective-permute-start.23 = (bf16[128,2048]{1,0:T(8,128)(2,1)S(1)}, bf16[128,2048]{1,0:T(8,128)(2,1)S(1)}, u32[]{:S(2)}, u32[]{:S(2)}) collective-permute-start(bf16[128,2048]{1,0:T(8,128)(2,1)S(1)} %get-tuple-element.43), channel_id=1, source_target_pairs={{0,17},{1,16},{8,25},{9,24},{16,1},{17,0},{24,9},{25,8},{2,19},{3,... | collective-permute-start | bytes 1572872 | tf_op jit(solution)/shard_map/ppermute | solution.py:22
  405.9 24.6 %collective-permute-start.22 = (bf16[128,2048]{1,0:T(8,128)(2,1)S(1)}, bf16[128,2048]{1,0:T(8,128)(2,1)S(1)}, u32[]{:S(2)}, u32[]{:S(2)}) collective-permute-start(bf16[128,2048]{1,0:T(8,128)(2,1)S(1)} %get-tuple-element.44), channel_id=1, source_target_pairs={{0,16},{1,17},{8,24},{9,25},{16,0},{17,1},{24,8},{25,9},{2,18},{3,... | collective-permute-start | bytes 1572872 | tf_op jit(solution)/shard_map/ppermute | solution.py:22
  408.9 41.4 %collective-permute-start.13 = (bf16[128,2048]{1,0:T(8,128)(2,1)S(1)}, bf16[128,2048]{1,0:T(8,128)(2,1)S(1)}, u32[]{:S(2)}, u32[]{:S(2)}) collective-permute-start(bf16[128,2048]{1,0:T(8,128)(2,1)S(1)} %get-tuple-element.45), channel_id=1, source_target_pairs={{0,1},{1,0},{8,9},{9,8},{16,17},{17,16},{24,25},{25,24},{2,3},{3,2... | collective-permute-start | bytes 1572872 | tf_op jit(solution)/shard_map/ppermute | solution.py:22
  410.5 39.8 %collective-permute-start.15 = (bf16[128,2048]{1,0:T(8,128)(2,1)S(1)}, bf16[128,2048]{1,0:T(8,128)(2,1)S(1)}, u32[]{:S(2)}, u32[]{:S(2)}) collective-permute-start(bf16[128,2048]{1,0:T(8,128)(2,1)S(1)} %get-tuple-element.46), channel_id=1, source_target_pairs={{0,17},{1,16},{8,25},{9,24},{16,1},{17,0},{24,9},{25,8},{2,19},{3,... | collective-permute-start | bytes 1572872 | tf_op jit(solution)/shard_map/ppermute | solution.py:22
  484.6 120.5 %reduce-scatter.7.cloned.1.call-start = ((), (), s32[]{:S(2)}) async-start(), calls=%async_computation.21 | async-start | bytes 5242880 | tf_op jit(solution)/shard_map/reduce_scatter | solution.py:217
  499.5 185.3 %reduce-scatter.5.cloned.1.call-start = ((), (), s32[]{:S(2)}) async-start(), calls=%async_computation.20 | async-start | bytes 5242880 | tf_op jit(solution)/shard_map/reduce_scatter | solution.py:217
  534.6 40.3 %collective-permute-start.29 = (bf16[128,2048]{1,0:T(8,128)(2,1)}, bf16[128,2048]{1,0:T(8,128)(2,1)}, u32[]{:S(2)}, u32[]{:S(2)}) collective-permute-start(bf16[128,2048]{1,0:T(8,128)(2,1)} %get-tuple-element.37), channel_id=1, source_target_pairs={{0,1},{1,0},{8,9},{9,8},{16,17},{17,16},{24,25},{25,24},{2,3},{3,2... | collective-permute-start | bytes 1572872 | tf_op jit(solution)/shard_map/ppermute | solution.py:22
  536.0 38.9 %collective-permute-start.31 = (bf16[128,2048]{1,0:T(8,128)(2,1)}, bf16[128,2048]{1,0:T(8,128)(2,1)}, u32[]{:S(2)}, u32[]{:S(2)}) collective-permute-start(bf16[128,2048]{1,0:T(8,128)(2,1)} %get-tuple-element.38), channel_id=1, source_target_pairs={{0,17},{1,16},{8,25},{9,24},{16,1},{17,0},{24,9},{25,8},{2,19},{3,... | collective-permute-start | bytes 1572872 | tf_op jit(solution)/shard_map/ppermute | solution.py:22
  537.6 37.4 %collective-permute-start.30 = (bf16[128,2048]{1,0:T(8,128)(2,1)}, bf16[128,2048]{1,0:T(8,128)(2,1)}, u32[]{:S(2)}, u32[]{:S(2)}) collective-permute-start(bf16[128,2048]{1,0:T(8,128)(2,1)} %get-tuple-element.39), channel_id=1, source_target_pairs={{0,16},{1,17},{8,24},{9,25},{16,0},{17,1},{24,8},{25,9},{2,18},{3,... | collective-permute-start | bytes 1572872 | tf_op jit(solution)/shard_map/ppermute | solution.py:22
  538.9 28.0 %all-to-all-start.5 = ((bf16[4,128,512]{2,1,0:T(8,128)(2,1)}), bf16[4,128,512]{2,1,0:T(8,128)(2,1)}, u32[]{:S(2)}, u32[]{:S(2)}) async-start(bf16[4,128,512]{2,1,0:T(8,128)(2,1)} %bitcast.451), calls=%async_computation.5 | async-start | bytes 1048576 | tf_op jit(solution)/shard_map/all_to_all | solution.py:41
  574.9 170.1 %all-gather.16.cloned.1.call-start = ((), (), s32[]{:S(2)}) async-start(), calls=%async_computation.24 | async-start | bytes 1081344 | tf_op jit(solution)/shard_map/all_gather | solution.py:300
  609.1 78.9 %all-to-all-start.9 = ((bf16[8,128,512]{2,1,0:T(8,128)(2,1)}), bf16[8,128,512]{2,1,0:T(8,128)(2,1)S(1)}, u32[]{:S(2)}, u32[]{:S(2)}) async-start(bf16[8,128,512]{2,1,0:T(8,128)(2,1)} %bitcast.126), calls=%async_computation.11 | async-start | bytes 2097152 | tf_op jit(solution)/shard_map/all_to_all | solution.py:258
  688.0 62.2 %all-to-all-start.8 = ((bf16[8,128,512]{2,1,0:T(8,128)(2,1)}), bf16[8,128,512]{2,1,0:T(8,128)(2,1)S(1)}, u32[]{:S(2)}, u32[]{:S(2)}) async-start(bf16[8,128,512]{2,1,0:T(8,128)(2,1)} %bitcast.116), calls=%async_computation.9 | async-start | bytes 2097152 | tf_op jit(solution)/shard_map/all_to_all | solution.py:258
  (75 other events, 652.8 us)
Sparse Core Ops, SparseCore 0:
  33.0 81.0 all-gather.7
  116.2 79.2 all-gather.9
  271.1 44.7 all-gather.11
  329.1 42.8 all-gather.13
  398.7 42.0 reduce-scatter.8
  484.7 41.8 reduce-scatter.10
  528.9 76.1 reduce-scatter.6
  607.5 77.2 reduce-scatter.4
  688.5 56.4 all-gather.15
